TPU v7x, 128 devices: a whole 4x4x4 slice. The times are simulated.
128 devices in a mesh: ctx: 32 (over x, y, core), tp: 4 (over z).
Axes of the slice: x: 4, y: 4, z: 4, core: 2. Of those that a mesh axis runs over, the one named last changes fastest.
Arguments:
- tokens: bfloat16 [16384, 4096], P('ctx'), may hold values from -6 to 6
- query_weight: bfloat16 [4096, 512], P(None, 'tp'), may hold values from -0.09375 to 0.09375
- key_weight: bfloat16 [4096, 512], P(None, 'tp'), may hold values from -0.09375 to 0.09375
- value_weight: bfloat16 [4096, 4096], P(None, 'tp'), may hold values from -0.09375 to 0.09375
- norm_gain: bfloat16 [4096], P('tp'), may hold values from 0.5 to 1.5
- out_weight: bfloat16 [4096, 4096], P('tp'), may hold values from -0.09375 to 0.09375
Outputs:
- attended: bfloat16 [16384, 4096], P('ctx', 'tp')
All inputs are finite; a program needn't handle non-finite values.
Results may differ from a plain program's by a relative error of at most 0.03.
Values may be sent and summed in bfloat16 or wider, within the bound.
A program may use at most 128 MiB of HBM per device.

v0:
```python
import jax
import jax.numpy as jnp
from jax import lax
from jax.sharding import PartitionSpec as P

F = 16
DV = 128


half_root = 0.7071067811865476


def passed_along(block, axis, distance):
    devices = range(lax.axis_size(axis))
    route = [(i - distance, i) for i in devices if i - distance in devices]
    return lax.ppermute(block, axis, route)


def project(inputs, weight, factor):
    return (jnp.dot(inputs, weight, preferred_element_type=jnp.float32) * factor).astype(
        jnp.bfloat16
    )


def pairs_of(features):
    rows, heads, width = features.shape
    wide = features.astype(jnp.float32)
    outer = wide[:, :, :, None] * wide[:, :, None, :] * half_root
    return outer.reshape(rows, heads, width * width).astype(jnp.bfloat16)


def add_states(earlier, later):
    return jax.tree.map(jnp.add, earlier, later)


def per_device(tokens, query_weight, key_weight, value_weight, norm_gain, out_weight):
    highest = lax.Precision.HIGHEST
    rows = tokens.shape[0]
    heads = norm_gain.shape[0] // DV
    factor = F ** (-0.25)
    query_rows = project(tokens, query_weight, factor).reshape(rows, heads, F)
    key_rows = project(tokens, key_weight, factor).reshape(rows, heads, F)
    value_rows = project(tokens, value_weight, 1.0).reshape(rows, heads, DV)
    query_pairs = pairs_of(query_rows)
    key_pairs = pairs_of(key_rows)
    local_states = (
        jnp.einsum("thp,thd->hpd", key_pairs, value_rows, preferred_element_type=jnp.float32),
        jnp.einsum("thf,thd->hfd", key_rows, value_rows, preferred_element_type=jnp.float32),
        jnp.sum(value_rows.astype(jnp.float32), axis=0),
        jnp.sum(key_pairs.astype(jnp.float32), axis=0),
        jnp.sum(key_rows.astype(jnp.float32), axis=0),
    )
    empty_states = jax.tree.map(jnp.zeros_like, local_states)

    def relay(turn_index, carried):
        summed = add_states(carried, local_states)
        return (
            passed_along(summed[0].astype(jnp.bfloat16), "ctx", 1).astype(jnp.float32),
            passed_along(summed[1].astype(jnp.bfloat16), "ctx", 1).astype(jnp.float32),
            passed_along(summed[2].astype(jnp.bfloat16), "ctx", 1).astype(jnp.float32),
            passed_along(summed[3].astype(jnp.bfloat16), "ctx", 1).astype(jnp.float32),
            passed_along(summed[4].astype(jnp.bfloat16), "ctx", 1).astype(jnp.float32),
        )

    prefix_states = lax.fori_loop(0, lax.axis_size("ctx") - 1, relay, empty_states)
    prev_pairs, prev_linear, prev_values, prev_pair_sums, prev_key_sums = prefix_states
    scores = jnp.einsum("thf,shf->hts", query_rows, key_rows, preferred_element_type=jnp.float32)
    causal_mask = jnp.tril(jnp.ones((rows, rows), jnp.float32)) > 0.5
    local_weights = jnp.where(causal_mask[None], 1.0 + scores + 0.5 * scores * scores, 0.0)
    rounded_weights = local_weights.astype(jnp.bfloat16)
    local_numerator = jnp.einsum(
        "hts,shd->thd", rounded_weights, value_rows, preferred_element_type=jnp.float32
    )
    local_denominator = jnp.transpose(jnp.sum(local_weights, axis=2))
    query_wide = query_rows.astype(jnp.float32)
    qpair_wide = query_pairs.astype(jnp.float32)
    numerator = prev_values[None] + jnp.einsum(
        "thf,hfd->thd", query_wide, prev_linear, precision=highest
    )
    numerator = numerator + jnp.einsum("thp,hpd->thd", qpair_wide, prev_pairs, precision=highest)
    numerator = numerator + local_numerator
    offset_count = lax.axis_index("ctx").astype(jnp.float32) * rows
    denominator = offset_count + jnp.einsum(
        "thf,hf->th", query_wide, prev_key_sums, precision=highest
    )
    denominator = denominator + jnp.einsum(
        "thp,hp->th", qpair_wide, prev_pair_sums, precision=highest
    )
    denominator = denominator + local_denominator
    ratio = numerator / denominator[:, :, None]
    spread = jnp.mean(ratio * ratio, axis=2, keepdims=True)
    gain_heads = norm_gain.astype(jnp.float32).reshape(heads, DV)
    normalized = (ratio / jnp.sqrt(spread + 1e-06) * gain_heads[None]).astype(jnp.bfloat16)
    normalized = normalized.reshape(rows, heads * DV)
    partial_value = jnp.dot(normalized, out_weight, preferred_element_type=jnp.float32)
    return lax.psum_scatter(
        partial_value.astype(jnp.bfloat16), "tp", scatter_dimension=1, tiled=True
    )


def solution(mesh):
    in_specs = (P("ctx", None), P(None, "tp"), P(None, "tp"), P(None, "tp"), P("tp"), P("tp", None))
    out_specs = P("ctx", "tp")
    return jax.shard_map(
        per_device, mesh=mesh, in_specs=in_specs, out_specs=out_specs, check_vma=False
    )
```

profile of v0, /device:TPU:1, one launch (start us, length us, event | category | flops | bytes accessed | tf_op | source)
XLA Modules:
  0.0 702.0 jit_solution(15351925278629091015)
XLA Ops:
  15.9 10.7 %convert_reduce_fusion.1 = (f32[1024]{0:T(1024)}, bf16[512,1024]{1,0:T(8,128)(2,1)}) fusion(bf16[512,4096]{1,0:T(8,128)(2,1)} %param.8, bf16[4096,1024]{1,0:T(8,128)(2,1)} %param.11), kind=kOutput, calls=%fused_computation.27 | convolution fusion | flops 4296539136 | bytes 13635584 | tf_op jit(solution)/shard_map/dot_general | solution.py:20
  37.3 583.8 %while.19 = (s32[]{:T(128)}, f32[8,256,128]{2,1,0:T(8,128)S(1)}, f32[8,16,128]{2,1,0:T(8,128)S(1)}, f32[8,128]{1,0:T(8,128)}, f32[8,256]{1,0:T(8,128)S(1)}, /*in...) while((s32[]{:T(128)}, f32[8,256,128]{2,1,0:T(8,128)S(1)}, ...), condition=%wide.region_4.0_spmd.clone, body=%wide.region_3.0_spmd.clone.sunk | while | flops 1126915 | bytes 6761811 | solution.py:65
  38.0 4.6 collective-permute-start.2
  85.0 4.2 collective-permute-start.3
  103.6 4.2 collective-permute-start.3
  120.0 5.1 collective-permute-start
  125.1 4.2 collective-permute-start.3
  143.7 4.2 collective-permute-start.3
  160.1 4.9 collective-permute-start
  165.0 4.2 collective-permute-start.3
  183.5 4.2 collective-permute-start.3
  202.1 4.2 collective-permute-start.3
  220.6 4.2 collective-permute-start.3
  239.2 4.2 collective-permute-start.3
  257.7 4.2 collective-permute-start.3
  276.3 4.2 collective-permute-start.3
  294.8 4.2 collective-permute-start.3
  313.4 4.2 collective-permute-start.3
  331.9 4.2 collective-permute-start.3
  350.4 4.2 collective-permute-start.3
  369.0 4.2 collective-permute-start.3
  387.5 4.2 collective-permute-start.3
  406.1 4.2 collective-permute-start.3
  424.6 4.2 collective-permute-start.3
  443.2 4.2 collective-permute-start.3
  461.7 4.2 collective-permute-start.3
  480.3 4.2 collective-permute-start.3
  498.8 4.2 collective-permute-start.3
  517.4 4.2 collective-permute-start.3
  535.9 4.2 collective-permute-start.3
  637.6 9.5 %convolution_convert_fusion = bf16[512,4096]{1,0:T(8,128)(2,1)} fusion(bf16[512,1024]{0,1:T(8,128)(2,1)S(1)} %bitcast.72, bf16[1024,4096]{1,0:T(8,128)(2,1)} %param.13), kind=kOutput, calls=%fused_computation.13 | convolution fusion | flops 4297064448 | bytes 13631488 | tf_op jit(solution)/shard_map/dot_general | solution.py:95
  647.1 48.0 %reduce-scatter.2.cloned.1.call-done = bf16[512,1024]{1,0:T(8,128)(2,1)} async-done(((bf16[512,4096]{1,0:T(8,128)(2,1)}), bf16[512,1024]{1,0:T(8,128)(2,1)}) %reduce-scatter.2.cloned.1.call-update) | async-done | bytes 1048592 | tf_op jit(solution)/shard_map/reduce_scatter | solution.py:96
  (643 shorter events, 497.8 us)
Async XLA Ops:
  6.5 688.6 %reduce-scatter.2.cloned.1.call-start = ((), (), s32[]{:S(2)}) async-start(), calls=%async_computation.1 | async-start | bytes 5242880 | tf_op jit(solution)/shard_map/reduce_scatter | solution.py:96
  38.0 17.0 %collective-permute-start.2 = (bf16[8,128]{1,0:T(8,128)(2,1)S(1)}, bf16[8,128]{1,0:T(8,128)(2,1)S(1)}, u32[]{:S(2)}, u32[]{:S(2)}) collective-permute-start(bf16[8,128]{1,0:T(8,128)(2,1)S(1)} %fusion.58), channel_id=1, source_target_pairs={{0,4},{4,8},{8,12},{12,16},{16,20},{20,24},{24,28},{28,32},{32,36}... | collective-permute-start | bytes 6152 | tf_op jit(solution)/shard_map/while/body/eval_jaxpr/ppermute | solution.py:16
  57.5 16.5 %collective-permute-start.2 = (bf16[8,128]{1,0:T(8,128)(2,1)S(1)}, bf16[8,128]{1,0:T(8,128)(2,1)S(1)}, u32[]{:S(2)}, u32[]{:S(2)}) collective-permute-start(bf16[8,128]{1,0:T(8,128)(2,1)S(1)} %fusion.58), channel_id=1, source_target_pairs={{0,4},{4,8},{8,12},{12,16},{16,20},{20,24},{24,28},{28,32},{32,36}... | collective-permute-start | bytes 6152 | tf_op jit(solution)/shard_map/while/body/eval_jaxpr/ppermute | solution.py:16
  76.4 17.8 %collective-permute-start.2 = (bf16[8,128]{1,0:T(8,128)(2,1)S(1)}, bf16[8,128]{1,0:T(8,128)(2,1)S(1)}, u32[]{:S(2)}, u32[]{:S(2)}) collective-permute-start(bf16[8,128]{1,0:T(8,128)(2,1)S(1)} %fusion.58), channel_id=1, source_target_pairs={{0,4},{4,8},{8,12},{12,16},{16,20},{20,24},{24,28},{28,32},{32,36}... | collective-permute-start | bytes 6152 | tf_op jit(solution)/shard_map/while/body/eval_jaxpr/ppermute | solution.py:16
  96.7 16.2 %collective-permute-start.2 = (bf16[8,128]{1,0:T(8,128)(2,1)S(1)}, bf16[8,128]{1,0:T(8,128)(2,1)S(1)}, u32[]{:S(2)}, u32[]{:S(2)}) collective-permute-start(bf16[8,128]{1,0:T(8,128)(2,1)S(1)} %fusion.58), channel_id=1, source_target_pairs={{0,4},{4,8},{8,12},{12,16},{16,20},{20,24},{24,28},{28,32},{32,36}... | collective-permute-start | bytes 6152 | tf_op jit(solution)/shard_map/while/body/eval_jaxpr/ppermute | solution.py:16
  115.3 19.0 %collective-permute-start.2 = (bf16[8,128]{1,0:T(8,128)(2,1)S(1)}, bf16[8,128]{1,0:T(8,128)(2,1)S(1)}, u32[]{:S(2)}, u32[]{:S(2)}) collective-permute-start(bf16[8,128]{1,0:T(8,128)(2,1)S(1)} %fusion.58), channel_id=1, source_target_pairs={{0,4},{4,8},{8,12},{12,16},{16,20},{20,24},{24,28},{28,32},{32,36}... | collective-permute-start | bytes 6152 | tf_op jit(solution)/shard_map/while/body/eval_jaxpr/ppermute | solution.py:16
  136.8 16.1 %collective-permute-start.2 = (bf16[8,128]{1,0:T(8,128)(2,1)S(1)}, bf16[8,128]{1,0:T(8,128)(2,1)S(1)}, u32[]{:S(2)}, u32[]{:S(2)}) collective-permute-start(bf16[8,128]{1,0:T(8,128)(2,1)S(1)} %fusion.58), channel_id=1, source_target_pairs={{0,4},{4,8},{8,12},{12,16},{16,20},{20,24},{24,28},{28,32},{32,36}... | collective-permute-start | bytes 6152 | tf_op jit(solution)/shard_map/while/body/eval_jaxpr/ppermute | solution.py:16
  155.4 18.8 %collective-permute-start.2 = (bf16[8,128]{1,0:T(8,128)(2,1)S(1)}, bf16[8,128]{1,0:T(8,128)(2,1)S(1)}, u32[]{:S(2)}, u32[]{:S(2)}) collective-permute-start(bf16[8,128]{1,0:T(8,128)(2,1)S(1)} %fusion.58), channel_id=1, source_target_pairs={{0,4},{4,8},{8,12},{12,16},{16,20},{20,24},{24,28},{28,32},{32,36}... | collective-permute-start | bytes 6152 | tf_op jit(solution)/shard_map/while/body/eval_jaxpr/ppermute | solution.py:16
  176.7 16.1 %collective-permute-start.2 = (bf16[8,128]{1,0:T(8,128)(2,1)S(1)}, bf16[8,128]{1,0:T(8,128)(2,1)S(1)}, u32[]{:S(2)}, u32[]{:S(2)}) collective-permute-start(bf16[8,128]{1,0:T(8,128)(2,1)S(1)} %fusion.58), channel_id=1, source_target_pairs={{0,4},{4,8},{8,12},{12,16},{16,20},{20,24},{24,28},{28,32},{32,36}... | collective-permute-start | bytes 6152 | tf_op jit(solution)/shard_map/while/body/eval_jaxpr/ppermute | solution.py:16
  195.2 16.1 %collective-permute-start.2 = (bf16[8,128]{1,0:T(8,128)(2,1)S(1)}, bf16[8,128]{1,0:T(8,128)(2,1)S(1)}, u32[]{:S(2)}, u32[]{:S(2)}) collective-permute-start(bf16[8,128]{1,0:T(8,128)(2,1)S(1)} %fusion.58), channel_id=1, source_target_pairs={{0,4},{4,8},{8,12},{12,16},{16,20},{20,24},{24,28},{28,32},{32,36}... | collective-permute-start | bytes 6152 | tf_op jit(solution)/shard_map/while/body/eval_jaxpr/ppermute | solution.py:16
  213.8 16.1 %collective-permute-start.2 = (bf16[8,128]{1,0:T(8,128)(2,1)S(1)}, bf16[8,128]{1,0:T(8,128)(2,1)S(1)}, u32[]{:S(2)}, u32[]{:S(2)}) collective-permute-start(bf16[8,128]{1,0:T(8,128)(2,1)S(1)} %fusion.58), channel_id=1, source_target_pairs={{0,4},{4,8},{8,12},{12,16},{16,20},{20,24},{24,28},{28,32},{32,36}... | collective-permute-start | bytes 6152 | tf_op jit(solution)/shard_map/while/body/eval_jaxpr/ppermute | solution.py:16
  232.3 16.1 %collective-permute-start.2 = (bf16[8,128]{1,0:T(8,128)(2,1)S(1)}, bf16[8,128]{1,0:T(8,128)(2,1)S(1)}, u32[]{:S(2)}, u32[]{:S(2)}) collective-permute-start(bf16[8,128]{1,0:T(8,128)(2,1)S(1)} %fusion.58), channel_id=1, source_target_pairs={{0,4},{4,8},{8,12},{12,16},{16,20},{20,24},{24,28},{28,32},{32,36}... | collective-permute-start | bytes 6152 | tf_op jit(solution)/shard_map/while/body/eval_jaxpr/ppermute | solution.py:16
  250.9 16.1 %collective-permute-start.2 = (bf16[8,128]{1,0:T(8,128)(2,1)S(1)}, bf16[8,128]{1,0:T(8,128)(2,1)S(1)}, u32[]{:S(2)}, u32[]{:S(2)}) collective-permute-start(bf16[8,128]{1,0:T(8,128)(2,1)S(1)} %fusion.58), channel_id=1, source_target_pairs={{0,4},{4,8},{8,12},{12,16},{16,20},{20,24},{24,28},{28,32},{32,36}... | collective-permute-start | bytes 6152 | tf_op jit(solution)/shard_map/while/body/eval_jaxpr/ppermute | solution.py:16
  269.4 16.1 %collective-permute-start.2 = (bf16[8,128]{1,0:T(8,128)(2,1)S(1)}, bf16[8,128]{1,0:T(8,128)(2,1)S(1)}, u32[]{:S(2)}, u32[]{:S(2)}) collective-permute-start(bf16[8,128]{1,0:T(8,128)(2,1)S(1)} %fusion.58), channel_id=1, source_target_pairs={{0,4},{4,8},{8,12},{12,16},{16,20},{20,24},{24,28},{28,32},{32,36}... | collective-permute-start | bytes 6152 | tf_op jit(solution)/shard_map/while/body/eval_jaxpr/ppermute | solution.py:16
  287.9 16.1 %collective-permute-start.2 = (bf16[8,128]{1,0:T(8,128)(2,1)S(1)}, bf16[8,128]{1,0:T(8,128)(2,1)S(1)}, u32[]{:S(2)}, u32[]{:S(2)}) collective-permute-start(bf16[8,128]{1,0:T(8,128)(2,1)S(1)} %fusion.58), channel_id=1, source_target_pairs={{0,4},{4,8},{8,12},{12,16},{16,20},{20,24},{24,28},{28,32},{32,36}... | collective-permute-start | bytes 6152 | tf_op jit(solution)/shard_map/while/body/eval_jaxpr/ppermute | solution.py:16
  306.5 16.1 %collective-permute-start.2 = (bf16[8,128]{1,0:T(8,128)(2,1)S(1)}, bf16[8,128]{1,0:T(8,128)(2,1)S(1)}, u32[]{:S(2)}, u32[]{:S(2)}) collective-permute-start(bf16[8,128]{1,0:T(8,128)(2,1)S(1)} %fusion.58), channel_id=1, source_target_pairs={{0,4},{4,8},{8,12},{12,16},{16,20},{20,24},{24,28},{28,32},{32,36}... | collective-permute-start | bytes 6152 | tf_op jit(solution)/shard_map/while/body/eval_jaxpr/ppermute | solution.py:16
  325.0 16.1 %collective-permute-start.2 = (bf16[8,128]{1,0:T(8,128)(2,1)S(1)}, bf16[8,128]{1,0:T(8,128)(2,1)S(1)}, u32[]{:S(2)}, u32[]{:S(2)}) collective-permute-start(bf16[8,128]{1,0:T(8,128)(2,1)S(1)} %fusion.58), channel_id=1, source_target_pairs={{0,4},{4,8},{8,12},{12,16},{16,20},{20,24},{24,28},{28,32},{32,36}... | collective-permute-start | bytes 6152 | tf_op jit(solution)/shard_map/while/body/eval_jaxpr/ppermute | solution.py:16
  343.6 16.1 %collective-permute-start.2 = (bf16[8,128]{1,0:T(8,128)(2,1)S(1)}, bf16[8,128]{1,0:T(8,128)(2,1)S(1)}, u32[]{:S(2)}, u32[]{:S(2)}) collective-permute-start(bf16[8,128]{1,0:T(8,128)(2,1)S(1)} %fusion.58), channel_id=1, source_target_pairs={{0,4},{4,8},{8,12},{12,16},{16,20},{20,24},{24,28},{28,32},{32,36}... | collective-permute-start | bytes 6152 | tf_op jit(solution)/shard_map/while/body/eval_jaxpr/ppermute | solution.py:16
  362.1 16.1 %collective-permute-start.2 = (bf16[8,128]{1,0:T(8,128)(2,1)S(1)}, bf16[8,128]{1,0:T(8,128)(2,1)S(1)}, u32[]{:S(2)}, u32[]{:S(2)}) collective-permute-start(bf16[8,128]{1,0:T(8,128)(2,1)S(1)} %fusion.58), channel_id=1, source_target_pairs={{0,4},{4,8},{8,12},{12,16},{16,20},{20,24},{24,28},{28,32},{32,36}... | collective-permute-start | bytes 6152 | tf_op jit(solution)/shard_map/while/body/eval_jaxpr/ppermute | solution.py:16
  380.7 16.1 %collective-permute-start.2 = (bf16[8,128]{1,0:T(8,128)(2,1)S(1)}, bf16[8,128]{1,0:T(8,128)(2,1)S(1)}, u32[]{:S(2)}, u32[]{:S(2)}) collective-permute-start(bf16[8,128]{1,0:T(8,128)(2,1)S(1)} %fusion.58), channel_id=1, source_target_pairs={{0,4},{4,8},{8,12},{12,16},{16,20},{20,24},{24,28},{28,32},{32,36}... | collective-permute-start | bytes 6152 | tf_op jit(solution)/shard_map/while/body/eval_jaxpr/ppermute | solution.py:16
  399.2 16.1 %collective-permute-start.2 = (bf16[8,128]{1,0:T(8,128)(2,1)S(1)}, bf16[8,128]{1,0:T(8,128)(2,1)S(1)}, u32[]{:S(2)}, u32[]{:S(2)}) collective-permute-start(bf16[8,128]{1,0:T(8,128)(2,1)S(1)} %fusion.58), channel_id=1, source_target_pairs={{0,4},{4,8},{8,12},{12,16},{16,20},{20,24},{24,28},{28,32},{32,36}... | collective-permute-start | bytes 6152 | tf_op jit(solution)/shard_map/while/body/eval_jaxpr/ppermute | solution.py:16
  417.8 16.1 %collective-permute-start.2 = (bf16[8,128]{1,0:T(8,128)(2,1)S(1)}, bf16[8,128]{1,0:T(8,128)(2,1)S(1)}, u32[]{:S(2)}, u32[]{:S(2)}) collective-permute-start(bf16[8,128]{1,0:T(8,128)(2,1)S(1)} %fusion.58), channel_id=1, source_target_pairs={{0,4},{4,8},{8,12},{12,16},{16,20},{20,24},{24,28},{28,32},{32,36}... | collective-permute-start | bytes 6152 | tf_op jit(solution)/shard_map/while/body/eval_jaxpr/ppermute | solution.py:16
  436.3 16.1 %collective-permute-start.2 = (bf16[8,128]{1,0:T(8,128)(2,1)S(1)}, bf16[8,128]{1,0:T(8,128)(2,1)S(1)}, u32[]{:S(2)}, u32[]{:S(2)}) collective-permute-start(bf16[8,128]{1,0:T(8,128)(2,1)S(1)} %fusion.58), channel_id=1, source_target_pairs={{0,4},{4,8},{8,12},{12,16},{16,20},{20,24},{24,28},{28,32},{32,36}... | collective-permute-start | bytes 6152 | tf_op jit(solution)/shard_map/while/body/eval_jaxpr/ppermute | solution.py:16
  454.9 16.1 %collective-permute-start.2 = (bf16[8,128]{1,0:T(8,128)(2,1)S(1)}, bf16[8,128]{1,0:T(8,128)(2,1)S(1)}, u32[]{:S(2)}, u32[]{:S(2)}) collective-permute-start(bf16[8,128]{1,0:T(8,128)(2,1)S(1)} %fusion.58), channel_id=1, source_target_pairs={{0,4},{4,8},{8,12},{12,16},{16,20},{20,24},{24,28},{28,32},{32,36}... | collective-permute-start | bytes 6152 | tf_op jit(solution)/shard_map/while/body/eval_jaxpr/ppermute | solution.py:16
  473.4 16.1 %collective-permute-start.2 = (bf16[8,128]{1,0:T(8,128)(2,1)S(1)}, bf16[8,128]{1,0:T(8,128)(2,1)S(1)}, u32[]{:S(2)}, u32[]{:S(2)}) collective-permute-start(bf16[8,128]{1,0:T(8,128)(2,1)S(1)} %fusion.58), channel_id=1, source_target_pairs={{0,4},{4,8},{8,12},{12,16},{16,20},{20,24},{24,28},{28,32},{32,36}... | collective-permute-start | bytes 6152 | tf_op jit(solution)/shard_map/while/body/eval_jaxpr/ppermute | solution.py:16
  492.0 16.1 %collective-permute-start.2 = (bf16[8,128]{1,0:T(8,128)(2,1)S(1)}, bf16[8,128]{1,0:T(8,128)(2,1)S(1)}, u32[]{:S(2)}, u32[]{:S(2)}) collective-permute-start(bf16[8,128]{1,0:T(8,128)(2,1)S(1)} %fusion.58), channel_id=1, source_target_pairs={{0,4},{4,8},{8,12},{12,16},{16,20},{20,24},{24,28},{28,32},{32,36}... | collective-permute-start | bytes 6152 | tf_op jit(solution)/shard_map/while/body/eval_jaxpr/ppermute | solution.py:16
  510.5 16.1 %collective-permute-start.2 = (bf16[8,128]{1,0:T(8,128)(2,1)S(1)}, bf16[8,128]{1,0:T(8,128)(2,1)S(1)}, u32[]{:S(2)}, u32[]{:S(2)}) collective-permute-start(bf16[8,128]{1,0:T(8,128)(2,1)S(1)} %fusion.58), channel_id=1, source_target_pairs={{0,4},{4,8},{8,12},{12,16},{16,20},{20,24},{24,28},{28,32},{32,36}... | collective-permute-start | bytes 6152 | tf_op jit(solution)/shard_map/while/body/eval_jaxpr/ppermute | solution.py:16
  529.0 16.1 %collective-permute-start.2 = (bf16[8,128]{1,0:T(8,128)(2,1)S(1)}, bf16[8,128]{1,0:T(8,128)(2,1)S(1)}, u32[]{:S(2)}, u32[]{:S(2)}) collective-permute-start(bf16[8,128]{1,0:T(8,128)(2,1)S(1)} %fusion.58), channel_id=1, source_target_pairs={{0,4},{4,8},{8,12},{12,16},{16,20},{20,24},{24,28},{28,32},{32,36}... | collective-permute-start | bytes 6152 | tf_op jit(solution)/shard_map/while/body/eval_jaxpr/ppermute | solution.py:16
  547.6 16.1 %collective-permute-start.2 = (bf16[8,128]{1,0:T(8,128)(2,1)S(1)}, bf16[8,128]{1,0:T(8,128)(2,1)S(1)}, u32[]{:S(2)}, u32[]{:S(2)}) collective-permute-start(bf16[8,128]{1,0:T(8,128)(2,1)S(1)} %fusion.58), channel_id=1, source_target_pairs={{0,4},{4,8},{8,12},{12,16},{16,20},{20,24},{24,28},{28,32},{32,36}... | collective-permute-start | bytes 6152 | tf_op jit(solution)/shard_map/while/body/eval_jaxpr/ppermute | solution.py:16
  566.1 16.1 %collective-permute-start.2 = (bf16[8,128]{1,0:T(8,128)(2,1)S(1)}, bf16[8,128]{1,0:T(8,128)(2,1)S(1)}, u32[]{:S(2)}, u32[]{:S(2)}) collective-permute-start(bf16[8,128]{1,0:T(8,128)(2,1)S(1)} %fusion.58), channel_id=1, source_target_pairs={{0,4},{4,8},{8,12},{12,16},{16,20},{20,24},{24,28},{28,32},{32,36}... | collective-permute-start | bytes 6152 | tf_op jit(solution)/shard_map/while/body/eval_jaxpr/ppermute | solution.py:16
  584.7 16.1 %collective-permute-start.2 = (bf16[8,128]{1,0:T(8,128)(2,1)S(1)}, bf16[8,128]{1,0:T(8,128)(2,1)S(1)}, u32[]{:S(2)}, u32[]{:S(2)}) collective-permute-start(bf16[8,128]{1,0:T(8,128)(2,1)S(1)} %fusion.58), channel_id=1, source_target_pairs={{0,4},{4,8},{8,12},{12,16},{16,20},{20,24},{24,28},{28,32},{32,36}... | collective-permute-start | bytes 6152 | tf_op jit(solution)/shard_map/while/body/eval_jaxpr/ppermute | solution.py:16
  603.2 16.1 %collective-permute-start.2 = (bf16[8,128]{1,0:T(8,128)(2,1)S(1)}, bf16[8,128]{1,0:T(8,128)(2,1)S(1)}, u32[]{:S(2)}, u32[]{:S(2)}) collective-permute-start(bf16[8,128]{1,0:T(8,128)(2,1)S(1)} %fusion.58), channel_id=1, source_target_pairs={{0,4},{4,8},{8,12},{12,16},{16,20},{20,24},{24,28},{28,32},{32,36}... | collective-permute-start | bytes 6152 | tf_op jit(solution)/shard_map/while/body/eval_jaxpr/ppermute | solution.py:16
  (135 other events, 1008.9 us)
Sparse Core Ops, SparseCore 0:
  647.3 47.8 reduce-scatter.1
where the time goes:
time: 709 us; the launch traced here: 702 us
  starting transfers between devices  442 us (62%)
  other arithmetic  113 us (16%)
  waiting for transfers between devices  82.3 us (12%)
  matrix products  45.7 us (6%)
  between operations  13.6 us (2%)
    ppermute x155, starting transfers between devices, passed_along(): return lax.ppermute(block, axis, route)  442 us
    reduce_scatter x1, waiting for transfers between devices, per_device(): lax.psum_scatter(partial_value.astype(jnp.bfloat16), 'tp', scatter_dimens...  48 us
    convert_element_type x31, other arithmetic, relay(): passed_along(summed[0].astype(jnp.bfloat16), 'ctx', 1).astype(jnp.float32)  34.5 us
    ppermute x155, waiting for transfers between devices, passed_along(): return lax.ppermute(block, axis, route)  34.3 us
    convert_element_type x31, other arithmetic, relay(): summed[0].astype(jnp.bfloat16)  28.6 us
    convert_element_type x31, other arithmetic, relay(): summed[2].astype(jnp.bfloat16)  22 us
    convert_element_type x31, other arithmetic, relay(): passed_along(summed[2].astype(jnp.bfloat16), 'ctx', 1).astype(jnp.float32)  18.3 us
    dot_general x3, matrix products, project(): jnp.dot(inputs, weight, preferred_element_type=jnp.float32) * factor  16.2 us
  transfers between devices with their start and end apart: 156, of which 32 were waited for; matrix products, arithmetic and copies ran while one was open for 7% of the time, Pallas kernels for 0%

commit v1 on v0

v1 whole, which is shorter than its diff:
```python
import functools

import jax
import jax.numpy as jnp
from jax import lax
from jax.experimental import pallas as pl
from jax.experimental.pallas import tpu as pltpu
from jax.sharding import PartitionSpec as P

MESH = pl.DeviceIdType.MESH
F = 16
DV = 128
HEADS = 8
HALF = 4
ROWS = 512
FEATS = 160
TILE = 256
RB = 4
RR = ROWS // RB
f32 = jnp.float32
bf16 = jnp.bfloat16


def iota(shape, axis):
    return lax.broadcasted_iota(jnp.int32, shape, axis)


def dot(a, b):
    return jnp.dot(a, b, preferred_element_type=f32)


def kernel(
    x_hbm, wq_hbm, wk_hbm, wv_hbm, gain_ref, wo_hbm, out_ref,
    x, wqk, wv, wo, q32, kt32, ktb, phi, vext, pick1, pick2, qext, acc, ps,
    send0, recv0, mine, send1, recv1, send2, recv2, send3, recv3,
    norm, far_s, far_r, near_s, near_r, comb, own,
    in_sem, wv_sem, wo_sem,
    s0, r0, s1, r1, s2, r2, s3, r3, fs, fr, ns, nr,
):
    ctx = lax.axis_index("ctx")
    z = lax.axis_index("tp")
    core = lax.rem(ctx, 2)
    cy = lax.rem(lax.div(ctx, 2), 4)
    cx = lax.div(ctx, 8)

    def at(px, py, pc, pz):
        return ((px * 4 + py) * 2 + pc, pz)

    partner = at(cx, cy, 1 - core, z)

    copies = [
        pltpu.make_async_copy(x_hbm, x, in_sem.at[0]),
        pltpu.make_async_copy(wk_hbm, wqk.at[:, pl.ds(128, 128)], in_sem.at[1]),
        pltpu.make_async_copy(wq_hbm, wqk.at[:, pl.ds(0, 128)], in_sem.at[2]),
    ]
    for c in copies:
        c.start()

    def wv_copy(i):
        block = lax.rem(2 * (1 - core) + i, 4)
        return pltpu.make_async_copy(
            wv_hbm.at[:, pl.ds(pl.multiple_of(block * 256, 256), 256)], wv.at[i], wv_sem.at[i]
        )

    def wo_copy(k):
        chunk = lax.rem(z + k, 4)
        return pltpu.make_async_copy(
            wo_hbm.at[:, pl.ds(pl.multiple_of(chunk * 1024, 1024), 1024)], wo.at[k], wo_sem.at[k]
        )

    for i in range(4):
        wv_copy(i).start()
    for k in (2, 1, 3, 0):
        wo_copy(k).start()

    barrier = pltpu.get_barrier_semaphore()
    peers = [partner]
    for d in (1, 2, 3):
        peers.append(at(lax.rem(cx + d, 4), cy, core, z))
        peers.append(at(cx, lax.rem(cy + d, 4), core, z))
    for d in (1, 3):
        peers.append(at(cx, cy, core, lax.rem(z + d, 4)))
    for p in peers:
        pl.semaphore_signal(barrier, inc=1, device_id=p, device_id_type=MESH)

    row = iota((256, FEATS), 0) - 112
    col = iota((256, FEATS), 1)
    low = col % 16
    first = jnp.where(col < 136, low, col - 136)
    second = (low + col // 16) % 16
    pick1[...] = jnp.where((row == first) & (col < 152), 1.0, 0.0).astype(bf16)
    pick2[...] = jnp.where((row == second) & (col < 136), 1.0, 0.0).astype(bf16)
    phi[:, pl.ds(FEATS, 256 - FEATS), :] = jnp.zeros((HEADS, 256 - FEATS, ROWS), bf16)
    vext[:, :, pl.ds(DV, DV)] = jnp.ones((HEADS, ROWS, DV), bf16)

    for c in copies:
        c.wait()
    qk = (dot(x[...], wqk[...]) * 0.5).astype(bf16).astype(f32)
    q32[...] = qk[:, 0:128]
    kt = qk[:, 128:256].T
    kt32[...] = kt
    ktb[...] = kt.astype(bf16)

    ones16 = jnp.ones((16, ROWS), bf16)

    def key_features(h, _):
        k = kt32[pl.ds(pl.multiple_of(h * 16, 16), 16), :]
        parts = [k * k * 0.5]
        for o in range(1, 8):
            parts.append(k * pltpu.roll(k, 16 - o, 0))
        parts.append(k[0:8] * k[8:16])
        parts.append(k)
        parts.append(jnp.where(iota((8, ROWS), 0) == 0, 1.0, 0.0))
        phi[h, pl.ds(0, FEATS), :] = jnp.concatenate(parts, axis=0).astype(bf16)
        return 0

    lax.fori_loop(0, HEADS, key_features, 0)

    def values(i):
        wv_copy(i).wait()
        block = lax.rem(2 * (1 - core) + i, 4)
        v = dot(x[...], wv[i]).astype(bf16)
        vext[2 * block, :, pl.ds(0, DV)] = v[:, 0:128]
        vext[2 * block + 1, :, pl.ds(0, DV)] = v[:, 128:256]

    def state(h):
        p = phi[h, pl.ds(0, FEATS), :]
        st = dot(p, vext[h, :, pl.ds(0, DV)])
        nt = (((1,), (1,)), ((), ()))
        sums0 = lax.dot_general(ones16, phi[h, pl.ds(0, 128), :], nt, preferred_element_type=f32)
        sums1 = lax.dot_general(ones16, phi[h, pl.ds(128, 128), :], nt, preferred_element_type=f32)
        i8 = iota((8, DV), 0)
        last = st[152:160] + jnp.where(i8 == 1, sums0[0:8], 0.0) + jnp.where(i8 == 2, sums1[0:8], 0.0)
        return jnp.concatenate([st[0:152], last], axis=0)

    other_base = HALF * (1 - core)
    my_base = HALF * core

    values(0)
    values(1)

    def other_states(i, _):
        send0[i] = state(other_base + i).astype(bf16)
        return 0

    lax.fori_loop(0, HALF, other_states, 0)

    pl.semaphore_wait(barrier, len(peers))

    def remote(src, dst, ss, rs, dev):
        return pltpu.make_async_remote_copy(
            src_ref=src, dst_ref=dst, send_sem=ss, recv_sem=rs, device_id=dev, device_id_type=MESH
        )

    copy0 = remote(send0, recv0, s0, r0, partner)
    copy0.start()

    values(2)
    values(3)

    def my_states(i, _):
        mine[i] = state(my_base + i)
        return 0

    lax.fori_loop(0, HALF, my_states, 0)
    copy0.wait_recv()
    send1[...] = (mine[pl.ds(0, HALF)] + recv0[...].astype(f32)).astype(bf16)

    pa = jnp.where(core == 0, cy, cx)
    pb = jnp.where(core == 0, cx, cy)

    def on_axes(a, b):
        return at(jnp.where(core == 0, b, a), jnp.where(core == 0, a, b), core, z)

    copies1 = []
    for n, d in enumerate((2, 1, 3)):
        copies1.append(remote(send1, recv1.at[n], s1.at[n], r1.at[n], on_axes(lax.rem(pa + d, 4), pb)))
    for c in copies1:
        c.start()

    c1 = jnp.where(iota((1, FEATS), 1) == 152, 1.0, 0.0)
    c2 = jnp.where((iota((1, FEATS), 1) >= 136) & (iota((1, FEATS), 1) <= 152), 1.0, 0.0)

    def local(h, _):
        q = q32[...]
        qm = jnp.where(iota((ROWS, 128), 1) // 16 == h, q, 0.0).astype(bf16)
        at_row = pl.ds(pl.multiple_of((7 - h) * 16, 16), 128)
        qb = q.astype(bf16)
        f1 = dot(qb, pick1[at_row, :]) + c1
        f2 = dot(qb, pick2[at_row, :]) + c2
        qext[h] = (f1 * f2).astype(bf16)
        below = iota((TILE, TILE), 1) <= iota((TILE, TILE), 0)
        for tb in range(ROWS // TILE):
            span = (tb + 1) * TILE
            r = dot(qm[tb * TILE : span], ktb[:, pl.ds(0, span)])
            w = (0.5 * r + 1.0) * r + 1.0
            diag = jnp.where(below, w[:, tb * TILE : span], 0.0).astype(bf16)
            a = dot(diag, vext[h, pl.ds(tb * TILE, TILE), :])
            if tb:
                a = a + dot(w[:, 0 : tb * TILE].astype(bf16), vext[h, pl.ds(0, tb * TILE), :])
            acc[h, pl.ds(tb * TILE, TILE), :] = a
        return 0

    lax.fori_loop(0, HALF, local, 0)

    for c in copies1:
        c.wait_recv()

    is1 = jnp.where(core == 1, 1.0, 0.0).astype(f32)
    senders = [lax.rem(pa + 4 - d, 4) for d in (2, 1, 3)]
    before = [jnp.where(s < pa, 1.0, 0.0).astype(f32) for s in senders]

    def sums_first(i, _):
        got = [recv1[n, i].astype(f32) for n in range(3)]
        mid = send1[i].astype(f32)
        pre = before[0] * got[0] + before[1] * got[1] + before[2] * got[2]
        every = got[0] + got[1] + got[2]
        send2[0, i] = (is1 * pre).astype(bf16)
        send2[1, i] = (mid + is1 * pre + (1.0 - is1) * every).astype(bf16)
        base = pre
        mine[i + HALF] = base
        return 0

    lax.fori_loop(0, HALF, sums_first, 0)

    copies2 = []
    for n, d in enumerate((2, 1, 3)):
        to = lax.rem(pb + d, 4)
        kind = jnp.where(to > pb, 1, 0)
        copies2.append(remote(send2.at[kind], recv2.at[n], s2.at[n], r2.at[n], on_axes(pa, to)))
    for c in copies2:
        c.start()

    lax.fori_loop(HALF, HEADS, local, 0)

    for c in copies2:
        c.wait_recv()

    def set_prefix(h, tile):
        ps[h, :, pl.ds(0, DV)] = tile.astype(bf16)
        rounded = tile[152:160]
        row0 = jnp.broadcast_to(rounded[1:2], (DV, DV))
        row1 = jnp.broadcast_to(rounded[2:3], (DV, DV))
        ps[h, pl.ds(0, 128), pl.ds(DV, DV)] = row0.T.astype(bf16)
        ps[h, pl.ds(128, 32), pl.ds(DV, DV)] = row1.T[0:32].astype(bf16)

    def sums_second(i, _):
        chips = mine[i + HALF] + recv2[0, i].astype(f32) + recv2[1, i].astype(f32) + recv2[2, i].astype(f32)
        send3[i] = (chips + (1.0 - is1) * mine[i]).astype(bf16)
        mine[i + HALF] = chips + is1 * recv0[i].astype(f32)
        return 0

    lax.fori_loop(0, HALF, sums_second, 0)
    copy3 = remote(send3, recv3, s3, r3, partner)
    copy3.start()

    def my_prefix(i, _):
        set_prefix(my_base + i, mine[i + HALF])
        return 0

    lax.fori_loop(0, HALF, my_prefix, 0)
    copy3.wait_recv()

    def other_prefix(i, _):
        set_prefix(other_base + i, recv3[i].astype(f32))
        return 0

    lax.fori_loop(0, HALF, other_prefix, 0)

    for k in range(4):
        wo_copy(k).wait()

    up = at(cx, cy, core, lax.rem(z + 1, 4))
    down = at(cx, cy, core, lax.rem(z + 3, 4))
    ways = (up, down)

    def far_copy(w, r):
        return remote(far_s.at[w, r], far_r.at[w, r], fs.at[w, r], fr.at[w, r], ways[w])

    def near_copy(w, kind, r):
        return remote(
            near_s.at[w, kind, r], near_r.at[w, kind, r], ns.at[w, kind, r], nr.at[w, kind, r], ways[w]
        )

    def rows_phase(r, _):
        at_rows = pl.ds(pl.multiple_of(r * RR, RR), RR)
        for h in range(HEADS):
            a = acc[h, at_rows, :] + dot(qext[h, at_rows, :], ps[h])
            ratio = a[:, 0:DV] / a[:, DV : 2 * DV]
            spread = jnp.mean(ratio * ratio, axis=1, keepdims=True)
            gain = gain_ref[:, pl.ds(h * DV, DV)].astype(f32)
            norm[:, pl.ds(h * DV, DV)] = (ratio * lax.rsqrt(spread + 1e-6) * gain).astype(bf16)

        def part(k, half):
            return dot(norm[...], wo[k, :, pl.ds(half * 512, 512)])

        for w in range(2):
            far_s[w, r] = part(2, w).astype(bf16)
            far_copy(w, r).start()
        near_s[0, 0, r] = part(1, 1).astype(bf16)
        near_copy(0, 0, r).start()
        near_s[1, 0, r] = part(3, 0).astype(bf16)
        near_copy(1, 0, r).start()
        comb[0, r] = part(1, 0)
        comb[1, r] = part(3, 1)
        own[r, :, pl.ds(0, 512)] = part(0, 0)
        own[r, :, pl.ds(512, 512)] = part(0, 1)
        return 0

    lax.fori_loop(0, RB, rows_phase, 0)

    def combine(r, _):
        for w in range(2):
            far_copy(w, r).wait_recv()
            near_s[w, 1, r] = (comb[w, r] + far_r[w, r].astype(f32)).astype(bf16)
            near_copy(w, 1, r).start()
        return 0

    lax.fori_loop(0, RB, combine, 0)

    def finish(r, _):
        for w in range(2):
            for kind in range(2):
                near_copy(w, kind, r).wait_recv()
        at_rows = pl.ds(pl.multiple_of(r * RR, RR), RR)
        left = own[r, :, pl.ds(0, 512)] + near_r[0, 1, r].astype(f32) + near_r[1, 0, r].astype(f32)
        right = own[r, :, pl.ds(512, 512)] + near_r[0, 0, r].astype(f32) + near_r[1, 1, r].astype(f32)
        out_ref[at_rows, pl.ds(0, 512)] = left.astype(bf16)
        out_ref[at_rows, pl.ds(512, 512)] = right.astype(bf16)
        return 0

    lax.fori_loop(0, RB, finish, 0)

    copy0.wait_send()
    for c in copies1 + copies2:
        c.wait_send()
    copy3.wait_send()

    def sent(r, _):
        for w in range(2):
            far_copy(w, r).wait_send()
            for kind in range(2):
                near_copy(w, kind, r).wait_send()
        return 0

    lax.fori_loop(0, RB, sent, 0)


def per_device(tokens, query_weight, key_weight, value_weight, norm_gain, out_weight):
    dma = pltpu.SemaphoreType.DMA
    hbm = pl.BlockSpec(memory_space=pl.ANY)
    vmem = pl.BlockSpec(memory_space=pltpu.VMEM)
    d = tokens.shape[1]
    return pl.pallas_call(
        kernel,
        out_shape=jax.ShapeDtypeStruct((ROWS, 1024), bf16),
        in_specs=[hbm, hbm, hbm, hbm, vmem, hbm],
        out_specs=vmem,
        scratch_shapes=[
            pltpu.VMEM((ROWS, d), bf16),
            pltpu.VMEM((d, 256), bf16),
            pltpu.VMEM((4, d, 256), bf16),
            pltpu.VMEM((4, 1024, 1024), bf16),
            pltpu.VMEM((ROWS, 128), f32),
            pltpu.VMEM((128, ROWS), f32),
            pltpu.VMEM((128, ROWS), bf16),
            pltpu.VMEM((HEADS, 256, ROWS), bf16),
            pltpu.VMEM((HEADS, ROWS, 2 * DV), bf16),
            pltpu.VMEM((256, FEATS), bf16),
            pltpu.VMEM((256, FEATS), bf16),
            pltpu.VMEM((HEADS, ROWS, FEATS), bf16),
            pltpu.VMEM((HEADS, ROWS, 2 * DV), f32),
            pltpu.VMEM((HEADS, FEATS, 2 * DV), bf16),
            pltpu.VMEM((HALF, FEATS, DV), bf16),
            pltpu.VMEM((HALF, FEATS, DV), bf16),
            pltpu.VMEM((2 * HALF, FEATS, DV), f32),
            pltpu.VMEM((HALF, FEATS, DV), bf16),
            pltpu.VMEM((3, HALF, FEATS, DV), bf16),
            pltpu.VMEM((2, HALF, FEATS, DV), bf16),
            pltpu.VMEM((3, HALF, FEATS, DV), bf16),
            pltpu.VMEM((HALF, FEATS, DV), bf16),
            pltpu.VMEM((HALF, FEATS, DV), bf16),
            pltpu.VMEM((RR, 1024), bf16),
            pltpu.VMEM((2, RB, RR, 512), bf16),
            pltpu.VMEM((2, RB, RR, 512), bf16),
            pltpu.VMEM((2, 2, RB, RR, 512), bf16),
            pltpu.VMEM((2, 2, RB, RR, 512), bf16),
            pltpu.VMEM((2, RB, RR, 512), f32),
            pltpu.VMEM((RB, RR, 1024), f32),
            dma((3,)),
            dma((4,)),
            dma((4,)),
            dma, dma, dma((3,)), dma((3,)), dma((3,)), dma((3,)), dma, dma,
            dma((2, RB)), dma((2, RB)), dma((2, 2, RB)), dma((2, 2, RB)),
        ],
        compiler_params=pltpu.CompilerParams(
            collective_id=0, has_side_effects=True, vmem_limit_bytes=60 * 1024 * 1024
        ),
    )(tokens, query_weight, key_weight, value_weight, norm_gain.reshape(1, -1), out_weight)


def solution(mesh):
    in_specs = (P("ctx", None), P(None, "tp"), P(None, "tp"), P(None, "tp"), P("tp"), P("tp", None))
    out_specs = P("ctx", "tp")
    return jax.shard_map(
        per_device, mesh=mesh, in_specs=in_specs, out_specs=out_specs, check_vma=False
    )
```

time: 709 us -> 83.1 us (0.12)
  starting transfers between devices: 442 us -> 0 us
  other arithmetic: 113 us -> 0 us
  waiting for transfers between devices: 82.3 us -> 0 us
  Pallas kernels: 0 us -> 79.4 us
  matrix products: 45.7 us -> 0 us
  between operations: 13.6 us -> 0.01 us
    ppermute x155 -> x0, starting transfers between devices: 442 us -> none  [passed_along(): return lax.ppermute(block, axis, route)]
    convert_element_type x313 -> x0, other arithmetic: 109 us -> none  [the longest x31 34.5 us: relay(): passed_along(summed[0].astype(jnp.bfloat16), 'ctx', 1).astype(jnp.float32)]
    pallas_call x0 -> x1, Pallas kernels: none -> 79.4 us  [per_device(): pl.pallas_call(kernel, out_shape=jax.ShapeDtypeStruct((ROWS, 1024), bf16)...]
    reduce_scatter x1 -> x0, waiting for transfers between devices: 48 us -> none  [per_device(): lax.psum_scatter(partial_value.astype(jnp.bfloat16), 'tp', scatter_dimens...]
    dot_general x12 -> x0, matrix products: 45.7 us -> none  [the longest x3 16.2 us: project(): jnp.dot(inputs, weight, preferred_element_type=jnp.float32) * factor]
    ppermute x155 -> x0, waiting for transfers between devices: 34.3 us -> none  [passed_along(): return lax.ppermute(block, axis, route)]
  transfers between devices with their start and end apart: 156 -> 0, of which waited for: 32 -> 0; matrix products, arithmetic and copies ran while one was open for 7% -> 0% of each run, Pallas kernels for 0% -> 0%
where the time goes in v1:
time: 83.1 us; the launch traced here: 82.9 us
  Pallas kernels  79.4 us (96%)
  local copies, waits for them, and re-layouts  3.54 us (4%)
    pallas_call x1, Pallas kernels, per_device(): pl.pallas_call(kernel, out_shape=jax.ShapeDtypeStruct((ROWS, 1024), bf16)...  79.4 us
    unnamed x1, local copies, waits for them, and re-layouts  2.26 us

profile of v1, /device:TPU:1, one launch (start us, length us, event | category | flops | bytes accessed | tf_op | source)
XLA Modules:
  0.0 82.9 jit_solution(13408907165563837350)
XLA Ops:
  0.0 1.3 %reshape.3.gain_ref = bf16[1,1024]{1,0:T(2,128)(2,1)} reshape(bf16[1024]{0:T(1024)(128)(2,1)} %param.10) | data formatting | bytes 4096 | tf_op jit(solution)/shard_map/reshape | solution.py:399
  1.3 79.4 %shard_map.64 = bf16[512,1024]{1,0:T(8,128)(2,1)} custom-call(bf16[512,4096]{1,0:T(8,128)(2,1)} %x_hbm.1, bf16[4096,128]{1,0:T(8,128)(2,1)} %wq_hbm.1, bf16[4096,128]{1,0:T(8,128)(2,1)} %wk_hbm.1, bf16[4096,1024]{1,0:T(8,128)(2,1)} %wv_hbm.1, bf16[1,1024]{1,0:T(2,128)(2,1)} %reshape.3.gain_ref, bf16[1024,4096]{1,0:T(8,128)(2,1)} %wo_hbm.1), custom_call_target="tpu_custom_call" | custom-call | tf_op jit(solution)/shard_map/pallas_call | solution.py:354
  80.6 2.3 %copy.8 = bf16[512,1024]{1,0:T(8,128)(2,1)} copy(bf16[512,1024]{1,0:T(8,128)(2,1)} %shard_map.64) | data formatting | bytes 2097152

commit v2 on v1

v2 whole, which is shorter than its diff:
```python
import functools

import jax
import jax.numpy as jnp
from jax import lax
from jax.experimental import pallas as pl
from jax.experimental.pallas import tpu as pltpu
from jax.sharding import PartitionSpec as P

MESH = pl.DeviceIdType.MESH
DV = 128
HEADS = 8
HALF = 4
ROWS = 512
FEATS = 160
TILE = 256
PAIR = 2
TURNS = (3, 6)
DISTANCES = (2, 1, 3)
SLOTS = ((2, 0), (2, 1), (1, 1), (3, 0), (1, 0), (3, 1), (0, 0), (0, 1))
RB = 4
RR = ROWS // RB
f32 = jnp.float32
bf16 = jnp.bfloat16


def iota(shape, axis):
    return lax.broadcasted_iota(jnp.int32, shape, axis)


def dot(a, b):
    return jnp.dot(a, b, preferred_element_type=f32)


def kernel(
    x_hbm, wq_hbm, wk_hbm, wv_hbm, gain_ref, wo_hbm, out_hbm,
    x, w, wo, proj, q32, kt32, ktb, phi, vext, pick1, pick2, qext, acc, ps,
    states, send0, recv0, send1, recv1, base, send2, recv2, send3, recv3,
    norm, zs, zr, part32, obuf,
    in_sem, w_sem, wo_sem, out_sem,
    s0, r0, s1, r1, s2, r2, s3, r3, zss, zrs,
):
    ctx = lax.axis_index("ctx")
    z = lax.axis_index("tp")
    core = lax.rem(ctx, 2)
    cy = lax.rem(lax.div(ctx, 2), 4)
    cx = lax.div(ctx, 8)

    def at(px, py, pc, pz):
        return ((px * 4 + py) * 2 + pc, pz)

    partner = at(cx, cy, 1 - core, z)

    x_copy = pltpu.make_async_copy(x_hbm, x, in_sem.at[0])
    k_copy = pltpu.make_async_copy(wk_hbm, w.at[0, :, pl.ds(128, 128)], in_sem.at[1])
    q_copy = pltpu.make_async_copy(wq_hbm, w.at[0, :, pl.ds(0, 128)], in_sem.at[2])
    for c in (x_copy, k_copy, q_copy):
        c.start()

    def block_of(i):
        return lax.rem(2 * (1 - core) + i - 1, 4)

    def wv_copy(i):
        columns = pl.ds(pl.multiple_of(block_of(i) * 256, 256), 256)
        return pltpu.make_async_copy(wv_hbm.at[:, columns], w.at[i], w_sem.at[i])

    for i in range(1, 5):
        wv_copy(i).start()

    def wo_copy(j):
        chunk, half = SLOTS[j]
        first = lax.rem(z + chunk, 4) * 1024 + half * 512
        columns = pl.ds(pl.multiple_of(first, 512), 512)
        return pltpu.make_async_copy(wo_hbm.at[:, columns], wo.at[j], wo_sem.at[j])

    barrier = pltpu.get_barrier_semaphore()
    peers = [partner]
    for d in (1, 2, 3):
        peers.append(at(lax.rem(cx + d, 4), cy, core, z))
        peers.append(at(cx, lax.rem(cy + d, 4), core, z))
    for d in (1, 3):
        peers.append(at(cx, cy, core, lax.rem(z + d, 4)))
    for p in peers:
        pl.semaphore_signal(barrier, inc=1, device_id=p, device_id_type=MESH)

    def remote(src, dst, ss, rs, dev):
        return pltpu.make_async_remote_copy(
            src_ref=src, dst_ref=dst, send_sem=ss, recv_sem=rs, device_id=dev, device_id_type=MESH
        )

    row = iota((256, FEATS), 0) - 112
    col = iota((256, FEATS), 1)
    low = col & 15
    first = jnp.where(col < 136, low, col - 136)
    second = (low + (col >> 4)) & 15
    pick1[...] = jnp.where((row == first) & (col < 152), 1.0, 0.0).astype(bf16)
    pick2[...] = jnp.where((row == second) & (col < 136), 1.0, 0.0).astype(bf16)
    phi[:, pl.ds(FEATS, 256 - FEATS), :] = jnp.zeros((HEADS, 256 - FEATS, ROWS), bf16)
    vext[:, :, pl.ds(DV, DV)] = jnp.ones((HEADS, ROWS, DV), bf16)

    ones16 = jnp.ones((16, ROWS), bf16)

    def key_features(h, _):
        k = kt32[pl.ds(pl.multiple_of(h * 16, 16), 16), :]
        parts = [k * k * 0.5]
        for o in range(1, 8):
            parts.append(k * pltpu.roll(k, 16 - o, 0))
        parts.append(k[0:8] * k[8:16])
        parts.append(k)
        parts.append(jnp.where(iota((8, ROWS), 0) == 0, 1.0, 0.0))
        phi[h, pl.ds(0, FEATS), :] = jnp.concatenate(parts, axis=0).astype(bf16)
        return 0

    def state(h):
        p = phi[h, pl.ds(0, FEATS), :]
        st = dot(p, vext[h, :, pl.ds(0, DV)])
        nt = (((1,), (1,)), ((), ()))
        sums0 = lax.dot_general(ones16, phi[h, pl.ds(0, 128), :], nt, preferred_element_type=f32)
        sums1 = lax.dot_general(ones16, phi[h, pl.ds(128, 128), :], nt, preferred_element_type=f32)
        i8 = iota((8, DV), 0)
        last = st[152:160] + jnp.where(i8 == 1, sums0[0:8], 0.0) + jnp.where(i8 == 2, sums1[0:8], 0.0)
        return jnp.concatenate([st[0:152], last], axis=0)

    pa = jnp.where(core == 0, cy, cx)
    pb = jnp.where(core == 0, cx, cy)

    def on_axes(a, b):
        return at(jnp.where(core == 0, b, a), jnp.where(core == 0, a, b), core, z)

    def copy0(c):
        return remote(send0.at[c], recv0.at[c], s0.at[c], r0.at[c], partner)

    def copies1(c):
        return [
            remote(send1.at[c], recv1.at[n, c], s1.at[n, c], r1.at[n, c], on_axes(lax.rem(pa + d, 4), pb))
            for n, d in enumerate(DISTANCES)
        ]

    def copies2(c):
        out = []
        for n, d in enumerate(DISTANCES):
            to = lax.rem(pb + d, 4)
            kind = jnp.where(to > pb, 1, 0)
            out.append(remote(send2.at[kind, c], recv2.at[n, c], s2.at[n, c], r2.at[n, c], on_axes(pa, to)))
        return out

    def copy3(c):
        return remote(send3.at[c], recv3.at[c], s3.at[c], r3.at[c], partner)

    def project(i, _):
        @pl.when(i == 0)
        def _():
            for c in (x_copy, k_copy, q_copy):
                c.wait()

        @pl.when(i > 0)
        def _():
            wv_copy(i).wait()

        def rows(m, _):
            at_rows = pl.ds(pl.multiple_of(m * TILE, TILE), TILE)
            proj[at_rows, :] = dot(x[at_rows, :], w[i])
            return 0

        lax.fori_loop(0, ROWS // TILE, rows, 0)

        @pl.when(i == 0)
        def _():
            qk = (proj[...] * 0.5).astype(bf16).astype(f32)
            q32[...] = qk[:, 0:128]
            kt = qk[:, 128:256].T
            kt32[...] = kt
            ktb[...] = kt.astype(bf16)
            lax.fori_loop(0, HEADS, key_features, 0)

        @pl.when(i > 0)
        def _():
            head = 2 * block_of(i)
            v = proj[...].astype(bf16)
            vext[head, :, pl.ds(0, DV)] = v[:, 0:128]
            vext[head + 1, :, pl.ds(0, DV)] = v[:, 128:256]

            def states_of(j, _):
                states[i - 1, j] = state(head + j)
                return 0

            lax.fori_loop(0, PAIR, states_of, 0)

        @pl.when(i == 1)
        def _():
            pl.semaphore_wait(barrier, len(peers))

        @pl.when((i == 1) | (i == 2))
        def _():
            c = i - 1
            send0[c] = states[c].astype(bf16)
            copy0(c).start()

        @pl.when(i >= 3)
        def _():
            c = i - 3
            copy0(c).wait_recv()
            send1[c] = (states[i - 1] + recv0[c].astype(f32)).astype(bf16)
            for k in copies1(c):
                k.start()

        @pl.when(i == 3)
        def _():
            for j in range(8):
                wo_copy(j).start()

        return 0

    lax.fori_loop(0, 5, project, 0)

    c1 = jnp.where(iota((1, FEATS), 1) == 152, 1.0, 0.0)
    c2 = jnp.where((iota((1, FEATS), 1) >= 136) & (iota((1, FEATS), 1) <= 152), 1.0, 0.0)
    is1 = jnp.where(core == 1, 1.0, 0.0).astype(f32)
    before = [jnp.where(lax.rem(pa + 4 - d, 4) < pa, 1.0, 0.0).astype(f32) for d in DISTANCES]

    def local(h, _):
        q = q32[...]
        qm = jnp.where((iota((ROWS, 128), 1) >> 4) == h, q, 0.0).astype(bf16)
        at_row = pl.ds(pl.multiple_of((7 - h) * 16, 16), 128)
        qb = q.astype(bf16)
        f1 = dot(qb, pick1[at_row, :]) + c1
        f2 = dot(qb, pick2[at_row, :]) + c2
        qext[h] = (f1 * f2).astype(bf16)
        below = iota((TILE, TILE), 1) <= iota((TILE, TILE), 0)
        for tb in range(ROWS // TILE):
            span = (tb + 1) * TILE
            r = dot(qm[tb * TILE : span], ktb[:, pl.ds(0, span)])
            wt = (0.5 * r + 1.0) * r + 1.0
            diag = jnp.where(below, wt[:, tb * TILE : span], 0.0).astype(bf16)
            a = dot(diag, vext[h, pl.ds(tb * TILE, TILE), :])
            if tb:
                a = a + dot(wt[:, 0 : tb * TILE].astype(bf16), vext[h, pl.ds(0, tb * TILE), :])
            acc[h, pl.ds(tb * TILE, TILE), :] = a

        @pl.when((h == TURNS[0]) | (h == TURNS[1]))
        def _():
            c = jnp.where(h == TURNS[1], 1, 0)
            for k in copies1(c):
                k.wait_recv()

            def sums_first(j, _):
                got = [recv1[n, c, j].astype(f32) for n in range(3)]
                pre = before[0] * got[0] + before[1] * got[1] + before[2] * got[2]
                every = got[0] + got[1] + got[2]
                send2[0, c, j] = (is1 * pre).astype(bf16)
                send2[1, c, j] = (send1[c, j].astype(f32) + is1 * pre + (1.0 - is1) * every).astype(bf16)
                base[c, j] = pre
                return 0

            lax.fori_loop(0, PAIR, sums_first, 0)
            for k in copies2(c):
                k.start()

        return 0

    lax.fori_loop(0, HEADS, local, 0)

    def set_prefix(h, tile):
        ps[h, :, pl.ds(0, DV)] = tile.astype(bf16)
        row0 = jnp.broadcast_to(tile[153:154], (DV, DV))
        row1 = jnp.broadcast_to(tile[154:155], (DV, DV))
        ps[h, pl.ds(0, 128), pl.ds(DV, DV)] = row0.T.astype(bf16)
        ps[h, pl.ds(128, 32), pl.ds(DV, DV)] = row1.T[0:32].astype(bf16)

    def second(c, _):
        for k in copies2(c):
            k.wait_recv()

        def sums_second(j, _):
            chips = base[c, j] + recv2[0, c, j].astype(f32) + recv2[1, c, j].astype(f32) + recv2[2, c, j].astype(f32)
            send3[c, j] = (chips + (1.0 - is1) * states[2 + c, j]).astype(bf16)
            base[c, j] = chips + is1 * recv0[c, j].astype(f32)
            return 0

        lax.fori_loop(0, PAIR, sums_second, 0)
        copy3(c).start()
        return 0

    lax.fori_loop(0, 2, second, 0)

    def prefixes(i, _):
        c = lax.div(lax.rem(i, 4), 2)
        j = lax.rem(i, 2)
        mine = i < 4

        @pl.when((i == 4) | (i == 6))
        def _():
            copy3(c).wait_recv()

        @pl.when(mine)
        def _():
            states[0, 0] = base[c, j]

        @pl.when(jnp.logical_not(mine))
        def _():
            states[0, 0] = recv3[c, j].astype(f32)

        half = jnp.where(mine, core, 1 - core)
        set_prefix(half * HALF + lax.rem(i, 4), states[0, 0])
        return 0

    lax.fori_loop(0, HEADS, prefixes, 0)

    for j in range(8):
        wo_copy(j).wait()

    def z_copy(j, r):
        to = lax.rem(z + 1 + 2 * lax.rem(j, 2), 4)
        return remote(zs.at[j, r], zr.at[j, r], zss.at[j, r], zrs.at[j, r], at(cx, cy, core, to))

    def rows_phase(r, _):
        at_rows = pl.ds(pl.multiple_of(r * RR, RR), RR)
        for h in range(HEADS):
            a = acc[h, at_rows, :] + dot(qext[h, at_rows, :], ps[h])
            ratio = a[:, 0:DV] / a[:, DV : 2 * DV]
            spread = jnp.mean(ratio * ratio, axis=1, keepdims=True)
            gain = gain_ref[:, pl.ds(h * DV, DV)].astype(f32)
            norm[:, pl.ds(h * DV, DV)] = (ratio * lax.rsqrt(spread + 1e-6) * gain).astype(bf16)

        def sent_parts(j, _):
            zs[j, r] = dot(norm[...], wo[j]).astype(bf16)
            z_copy(j, r).start()
            return 0

        lax.fori_loop(0, 4, sent_parts, 0)

        def kept_parts(j, _):
            part32[j, r] = dot(norm[...], wo[4 + j])
            return 0

        lax.fori_loop(0, 4, kept_parts, 0)
        return 0

    lax.fori_loop(0, RB, rows_phase, 0)

    def combine(r, _):
        for way in range(2):
            z_copy(way, r).wait_recv()
            zs[4 + way, r] = (part32[way, r] + zr[way, r].astype(f32)).astype(bf16)
            z_copy(4 + way, r).start()
        return 0

    lax.fori_loop(0, RB, combine, 0)

    def out_copy(r):
        at_rows = pl.ds(pl.multiple_of(r * RR, RR), RR)
        return pltpu.make_async_copy(obuf.at[r], out_hbm.at[at_rows, :], out_sem.at[r])

    def finish(r, _):
        for j in range(2, 6):
            z_copy(j, r).wait_recv()
        left = part32[2, r] + zr[4, r].astype(f32) + zr[3, r].astype(f32)
        right = part32[3, r] + zr[2, r].astype(f32) + zr[5, r].astype(f32)
        obuf[r, :, pl.ds(0, 512)] = left.astype(bf16)
        obuf[r, :, pl.ds(512, 512)] = right.astype(bf16)
        out_copy(r).start()
        return 0

    lax.fori_loop(0, RB, finish, 0)

    def drain(c, _):
        copy0(c).wait_send()
        copy3(c).wait_send()
        for k in copies1(c) + copies2(c):
            k.wait_send()
        return 0

    lax.fori_loop(0, 2, drain, 0)

    def sent(r, _):
        for j in range(6):
            z_copy(j, r).wait_send()
        out_copy(r).wait()
        return 0

    lax.fori_loop(0, RB, sent, 0)


def per_device(tokens, query_weight, key_weight, value_weight, norm_gain, out_weight):
    dma = pltpu.SemaphoreType.DMA
    hbm = pl.BlockSpec(memory_space=pl.ANY)
    vmem = pl.BlockSpec(memory_space=pltpu.VMEM)
    d = tokens.shape[1]
    tiles = (PAIR, FEATS, DV)
    return pl.pallas_call(
        kernel,
        out_shape=jax.ShapeDtypeStruct((ROWS, 1024), bf16),
        in_specs=[hbm, hbm, hbm, hbm, vmem, hbm],
        out_specs=hbm,
        scratch_shapes=[
            pltpu.VMEM((ROWS, d), bf16),
            pltpu.VMEM((5, d, 256), bf16),
            pltpu.VMEM((8, 1024, 512), bf16),
            pltpu.VMEM((ROWS, 256), f32),
            pltpu.VMEM((ROWS, 128), f32),
            pltpu.VMEM((128, ROWS), f32),
            pltpu.VMEM((128, ROWS), bf16),
            pltpu.VMEM((HEADS, 256, ROWS), bf16),
            pltpu.VMEM((HEADS, ROWS, 2 * DV), bf16),
            pltpu.VMEM((256, FEATS), bf16),
            pltpu.VMEM((256, FEATS), bf16),
            pltpu.VMEM((HEADS, ROWS, FEATS), bf16),
            pltpu.VMEM((HEADS, ROWS, 2 * DV), f32),
            pltpu.VMEM((HEADS, FEATS, 2 * DV), bf16),
            pltpu.VMEM((4,) + tiles, f32),
            pltpu.VMEM((2,) + tiles, bf16),
            pltpu.VMEM((2,) + tiles, bf16),
            pltpu.VMEM((2,) + tiles, bf16),
            pltpu.VMEM((3, 2) + tiles, bf16),
            pltpu.VMEM((2,) + tiles, f32),
            pltpu.VMEM((2, 2) + tiles, bf16),
            pltpu.VMEM((3, 2) + tiles, bf16),
            pltpu.VMEM((2,) + tiles, bf16),
            pltpu.VMEM((2,) + tiles, bf16),
            pltpu.VMEM((RR, 1024), bf16),
            pltpu.VMEM((6, RB, RR, 512), bf16),
            pltpu.VMEM((6, RB, RR, 512), bf16),
            pltpu.VMEM((4, RB, RR, 512), f32),
            pltpu.VMEM((RB, RR, 1024), bf16),
            dma((3,)),
            dma((5,)),
            dma((8,)),
            dma((RB,)),
            dma((2,)), dma((2,)), dma((3, 2)), dma((3, 2)), dma((3, 2)), dma((3, 2)), dma((2,)), dma((2,)),
            dma((6, RB)), dma((6, RB)),
        ],
        compiler_params=pltpu.CompilerParams(
            collective_id=0, has_side_effects=True, vmem_limit_bytes=56 * 1024 * 1024
        ),
    )(tokens, query_weight, key_weight, value_weight, norm_gain.reshape(1, -1), out_weight)


def solution(mesh):
    in_specs = (P("ctx", None), P(None, "tp"), P(None, "tp"), P(None, "tp"), P("tp"), P("tp", None))
    out_specs = P("ctx", "tp")
    return jax.shard_map(
        per_device, mesh=mesh, in_specs=in_specs, out_specs=out_specs, check_vma=False
    )
```

time: 83.1 us -> 73 us (0.88)
  Pallas kernels: 79.4 us -> 69.2 us
    pallas_call x1, Pallas kernels: 79.4 us -> 69.2 us  [per_device(): pl.pallas_call(kernel, out_shape=jax.ShapeDtypeStruct((ROWS, 1024), bf16)...]
where the time goes in v2:
time: 73 us; the launch traced here: 72.8 us
  Pallas kernels  69.2 us (95%)
  local copies, waits for them, and re-layouts  3.54 us (5%)
    pallas_call x1, Pallas kernels, per_device(): pl.pallas_call(kernel, out_shape=jax.ShapeDtypeStruct((ROWS, 1024), bf16)...  69.2 us
    unnamed x1, local copies, waits for them, and re-layouts  2.26 us

profile of v2, /device:TPU:1, one launch (start us, length us, event | category | flops | bytes accessed | tf_op | source)
XLA Modules:
  0.0 72.8 jit_solution(259690032999803824)
XLA Ops:
  0.0 1.3 %reshape.3.gain_ref = bf16[1,1024]{1,0:T(2,128)(2,1)} reshape(bf16[1024]{0:T(1024)(128)(2,1)} %param.10) | data formatting | bytes 4096 | tf_op jit(solution)/shard_map/reshape | solution.py:435
  1.3 69.2 %shard_map.64 = bf16[512,1024]{1,0:T(8,128)(2,1)} custom-call(bf16[512,4096]{1,0:T(8,128)(2,1)} %x_hbm.1, bf16[4096,128]{1,0:T(8,128)(2,1)} %wq_hbm.1, bf16[4096,128]{1,0:T(8,128)(2,1)} %wk_hbm.1, bf16[4096,1024]{1,0:T(8,128)(2,1)} %wv_hbm.1, bf16[1,1024]{1,0:T(2,128)(2,1)} %reshape.3.gain_ref, bf16[1024,4096]{1,0:T(8,128)(2,1)} %wo_hbm.1), custom_call_target="tpu_custom_call" | custom-call | tf_op jit(solution)/shard_map/pallas_call | solution.py:390
  70.5 2.3 %copy.8 = bf16[512,1024]{1,0:T(8,128)(2,1)} copy(bf16[512,1024]{1,0:T(8,128)(2,1)} %shard_map.64) | data formatting | bytes 2097152

commit v3 on v2

--- a/solution.py
+++ b/solution.py
@@ -36,7 +36,7 @@
     x_hbm, wq_hbm, wk_hbm, wv_hbm, gain_ref, wo_hbm, out_hbm,
     x, w, wo, proj, q32, kt32, ktb, phi, vext, pick1, pick2, qext, acc, ps,
     states, send0, recv0, send1, recv1, base, send2, recv2, send3, recv3,
-    norm, zs, zr, part32, obuf,
+    norm, gains, zs, zr, part32, obuf,
     in_sem, w_sem, wo_sem, out_sem,
     s0, r0, s1, r1, s2, r2, s3, r3, zss, zrs,
 ):
@@ -96,6 +96,9 @@
     pick1[...] = jnp.where((row == first) & (col < 152), 1.0, 0.0).astype(bf16)
     pick2[...] = jnp.where((row == second) & (col < 136), 1.0, 0.0).astype(bf16)
     phi[:, pl.ds(FEATS, 256 - FEATS), :] = jnp.zeros((HEADS, 256 - FEATS, ROWS), bf16)
+    for h in range(HEADS):
+        at_head = pl.ds(h * DV, DV)
+        gains[0:1, at_head] = gain_ref[at_head].astype(f32).reshape(1, DV)
     vext[:, :, pl.ds(DV, DV)] = jnp.ones((HEADS, ROWS, DV), bf16)
 
     ones16 = jnp.ones((16, ROWS), bf16)
@@ -115,10 +118,9 @@
         p = phi[h, pl.ds(0, FEATS), :]
         st = dot(p, vext[h, :, pl.ds(0, DV)])
         nt = (((1,), (1,)), ((), ()))
-        sums0 = lax.dot_general(ones16, phi[h, pl.ds(0, 128), :], nt, preferred_element_type=f32)
-        sums1 = lax.dot_general(ones16, phi[h, pl.ds(128, 128), :], nt, preferred_element_type=f32)
+        sums = lax.dot_general(ones16, phi[h], nt, preferred_element_type=f32)
         i8 = iota((8, DV), 0)
-        last = st[152:160] + jnp.where(i8 == 1, sums0[0:8], 0.0) + jnp.where(i8 == 2, sums1[0:8], 0.0)
+        last = st[152:160] + jnp.where(i8 == 1, sums[0:8, 0:DV], 0.0) + jnp.where(i8 == 2, sums[0:8, DV:], 0.0)
         return jnp.concatenate([st[0:152], last], axis=0)
 
     pa = jnp.where(core == 0, cy, cx)
@@ -130,19 +132,47 @@
     def copy0(c):
         return remote(send0.at[c], recv0.at[c], s0.at[c], r0.at[c], partner)
 
+    def needed1(sender, receiver):
+        return (core == 0) | (sender < receiver)
+
+    def needed2(sender, receiver):
+        return (core == 1) | (sender < receiver)
+
     def copies1(c):
-        return [
-            remote(send1.at[c], recv1.at[n, c], s1.at[n, c], r1.at[n, c], on_axes(lax.rem(pa + d, 4), pb))
-            for n, d in enumerate(DISTANCES)
-        ]
+        out = []
+        for n, d in enumerate(DISTANCES):
+            to, source = lax.rem(pa + d, 4), lax.rem(pa + 4 - d, 4)
+            copy = remote(send1.at[c], recv1.at[n, c], s1.at[n, c], r1.at[n, c], on_axes(to, pb))
+            out.append((copy, needed1(pa, to), needed1(source, pa)))
+        return out
 
     def copies2(c):
         out = []
         for n, d in enumerate(DISTANCES):
-            to = lax.rem(pb + d, 4)
+            to, source = lax.rem(pb + d, 4), lax.rem(pb + 4 - d, 4)
             kind = jnp.where(to > pb, 1, 0)
-            out.append(remote(send2.at[kind, c], recv2.at[n, c], s2.at[n, c], r2.at[n, c], on_axes(pa, to)))
+            copy = remote(send2.at[kind, c], recv2.at[n, c], s2.at[n, c], r2.at[n, c], on_axes(pa, to))
+            out.append((copy, needed2(pb, to), needed2(source, pb)))
         return out
+
+    def start(copies):
+        for copy, sends, _ in copies:
+            pl.when(sends)(copy.start)
+
+    def wait_recv(copies):
+        for copy, _, receives in copies:
+            pl.when(receives)(copy.wait_recv)
+
+    def wait_send(copies):
+        for copy, sends, _ in copies:
+            pl.when(sends)(copy.wait_send)
+
+    for buffer, copies in ((recv1, copies1(0)), (recv2, copies2(0))):
+        for n, (_, _, receives) in enumerate(copies):
+
+            @pl.when(jnp.logical_not(receives))
+            def _():
+                buffer[n] = jnp.zeros((2, PAIR, FEATS, DV), bf16)
 
     def copy3(c):
         return remote(send3.at[c], recv3.at[c], s3.at[c], r3.at[c], partner)
@@ -201,8 +231,7 @@
             c = i - 3
             copy0(c).wait_recv()
             send1[c] = (states[i - 1] + recv0[c].astype(f32)).astype(bf16)
-            for k in copies1(c):
-                k.start()
+            start(copies1(c))
 
         @pl.when(i == 3)
         def _():
@@ -240,8 +269,7 @@
         @pl.when((h == TURNS[0]) | (h == TURNS[1]))
         def _():
             c = jnp.where(h == TURNS[1], 1, 0)
-            for k in copies1(c):
-                k.wait_recv()
+            wait_recv(copies1(c))
 
             def sums_first(j, _):
                 got = [recv1[n, c, j].astype(f32) for n in range(3)]
@@ -253,8 +281,7 @@
                 return 0
 
             lax.fori_loop(0, PAIR, sums_first, 0)
-            for k in copies2(c):
-                k.start()
+            start(copies2(c))
 
         return 0
 
@@ -267,9 +294,15 @@
         ps[h, pl.ds(0, 128), pl.ds(DV, DV)] = row0.T.astype(bf16)
         ps[h, pl.ds(128, 32), pl.ds(DV, DV)] = row1.T[0:32].astype(bf16)
 
+    def normalize(h, at_rows):
+        at_head = pl.ds(pl.multiple_of(h * DV, DV), DV)
+        a = acc[h, at_rows, :] + dot(qext[h, at_rows, :], ps[h])
+        ratio = a[:, 0:DV] / a[:, DV : 2 * DV]
+        spread = jnp.mean(ratio * ratio, axis=1, keepdims=True)
+        norm[at_rows, at_head] = (ratio * lax.rsqrt(spread + 1e-6) * gains[0:1, at_head]).astype(bf16)
+
     def second(c, _):
-        for k in copies2(c):
-            k.wait_recv()
+        wait_recv(copies2(c))
 
         def sums_second(j, _):
             chips = base[c, j] + recv2[0, c, j].astype(f32) + recv2[1, c, j].astype(f32) + recv2[2, c, j].astype(f32)
@@ -279,32 +312,29 @@
 
         lax.fori_loop(0, PAIR, sums_second, 0)
         copy3(c).start()
+
+        def own_prefix(j, _):
+            h = core * HALF + c * PAIR + j
+            set_prefix(h, base[c, j])
+            normalize(h, pl.ds(0, ROWS))
+            return 0
+
+        lax.fori_loop(0, PAIR, own_prefix, 0)
         return 0
 
     lax.fori_loop(0, 2, second, 0)
 
     def prefixes(i, _):
-        c = lax.div(lax.rem(i, 4), 2)
-        j = lax.rem(i, 2)
-        mine = i < 4
-
-        @pl.when((i == 4) | (i == 6))
+        c, j = lax.div(i, 2), lax.rem(i, 2)
+
+        @pl.when(j == 0)
         def _():
             copy3(c).wait_recv()
 
-        @pl.when(mine)
-        def _():
-            states[0, 0] = base[c, j]
-
-        @pl.when(jnp.logical_not(mine))
-        def _():
-            states[0, 0] = recv3[c, j].astype(f32)
-
-        half = jnp.where(mine, core, 1 - core)
-        set_prefix(half * HALF + lax.rem(i, 4), states[0, 0])
-        return 0
-
-    lax.fori_loop(0, HEADS, prefixes, 0)
+        set_prefix((1 - core) * HALF + i, recv3[c, j].astype(f32))
+        return 0
+
+    lax.fori_loop(0, HALF, prefixes, 0)
 
     for j in range(8):
         wo_copy(j).wait()
@@ -315,22 +345,18 @@
 
     def rows_phase(r, _):
         at_rows = pl.ds(pl.multiple_of(r * RR, RR), RR)
-        for h in range(HEADS):
-            a = acc[h, at_rows, :] + dot(qext[h, at_rows, :], ps[h])
-            ratio = a[:, 0:DV] / a[:, DV : 2 * DV]
-            spread = jnp.mean(ratio * ratio, axis=1, keepdims=True)
-            gain = gain_ref[:, pl.ds(h * DV, DV)].astype(f32)
-            norm[:, pl.ds(h * DV, DV)] = (ratio * lax.rsqrt(spread + 1e-6) * gain).astype(bf16)
+        for i in range(HALF):
+            normalize((1 - core) * HALF + i, at_rows)
 
         def sent_parts(j, _):
-            zs[j, r] = dot(norm[...], wo[j]).astype(bf16)
+            zs[j, r] = dot(norm[at_rows, :], wo[j]).astype(bf16)
             z_copy(j, r).start()
             return 0
 
         lax.fori_loop(0, 4, sent_parts, 0)
 
         def kept_parts(j, _):
-            part32[j, r] = dot(norm[...], wo[4 + j])
+            part32[j, r] = dot(norm[at_rows, :], wo[4 + j])
             return 0
 
         lax.fori_loop(0, 4, kept_parts, 0)
@@ -366,8 +392,8 @@
     def drain(c, _):
         copy0(c).wait_send()
         copy3(c).wait_send()
-        for k in copies1(c) + copies2(c):
-            k.wait_send()
+        wait_send(copies1(c))
+        wait_send(copies2(c))
         return 0
 
     lax.fori_loop(0, 2, drain, 0)
@@ -383,7 +409,7 @@
 
 def per_device(tokens, query_weight, key_weight, value_weight, norm_gain, out_weight):
     dma = pltpu.SemaphoreType.DMA
-    hbm = pl.BlockSpec(memory_space=pl.ANY)
+    hbm = pl.BlockSpec(memory_space=pltpu.HBM)
     vmem = pl.BlockSpec(memory_space=pltpu.VMEM)
     d = tokens.shape[1]
     tiles = (PAIR, FEATS, DV)
@@ -391,7 +417,7 @@
         kernel,
         out_shape=jax.ShapeDtypeStruct((ROWS, 1024), bf16),
         in_specs=[hbm, hbm, hbm, hbm, vmem, hbm],
-        out_specs=hbm,
+        out_specs=pl.BlockSpec(memory_space=pl.ANY),
         scratch_shapes=[
             pltpu.VMEM((ROWS, d), bf16),
             pltpu.VMEM((5, d, 256), bf16),
@@ -417,7 +443,8 @@
             pltpu.VMEM((3, 2) + tiles, bf16),
             pltpu.VMEM((2,) + tiles, bf16),
             pltpu.VMEM((2,) + tiles, bf16),
-            pltpu.VMEM((RR, 1024), bf16),
+            pltpu.VMEM((ROWS, 1024), bf16),
+            pltpu.VMEM((8, 1024), f32),
             pltpu.VMEM((6, RB, RR, 512), bf16),
             pltpu.VMEM((6, RB, RR, 512), bf16),
             pltpu.VMEM((4, RB, RR, 512), f32),
@@ -430,9 +457,9 @@
             dma((6, RB)), dma((6, RB)),
         ],
         compiler_params=pltpu.CompilerParams(
-            collective_id=0, has_side_effects=True, vmem_limit_bytes=56 * 1024 * 1024
+            collective_id=0, has_side_effects=True, vmem_limit_bytes=52 * 1024 * 1024
         ),
-    )(tokens, query_weight, key_weight, value_weight, norm_gain.reshape(1, -1), out_weight)
+    )(tokens, query_weight, key_weight, value_weight, norm_gain, out_weight)
 
 
 def solution(mesh):

time: 73 us -> 66.5 us (0.911)
  Pallas kernels: 69.2 us -> 64.8 us
  local copies, waits for them, and re-layouts: 3.54 us -> 1.65 us
    pallas_call x1, Pallas kernels: 69.2 us -> 64.8 us  [per_device(): pl.pallas_call(kernel, out_shape=jax.ShapeDtypeStruct((ROWS, 1024), bf16)...]
    reshape x1 -> x0, local copies, waits for them, and re-layouts: 1.28 us -> none  [per_device(): norm_gain.reshape(1, -1)]
    unnamed x1 -> x3, local copies, waits for them, and re-layouts: 2.26 us -> 1.65 us
where the time goes in v3:
time: 66.5 us; the launch traced here: 66.4 us
  Pallas kernels  64.8 us (97%)
  local copies, waits for them, and re-layouts  1.65 us (2%)
    pallas_call x1, Pallas kernels, per_device(): pl.pallas_call(kernel, out_shape=jax.ShapeDtypeStruct((ROWS, 1024), bf16)...  64.8 us
    unnamed x3, local copies, waits for them, and re-layouts  1.65 us

profile of v3, /device:TPU:1, one launch (start us, length us, event | category | flops | bytes accessed | tf_op | source)
XLA Modules:
  0.0 66.4 jit_solution(13676486730223248324)
XLA Ops:
  0.0 0.0 copy-start
  0.0 0.7 %copy-done = bf16[1024]{0:T(1024)(128)(2,1)S(1)} copy-done((bf16[1024]{0:T(1024)(128)(2,1)S(1)}, bf16[1024]{0:T(1024)(128)(2,1)}, u32[]{:S(2)}) %copy-start) | copy-done | bytes 2072
  0.7 64.8 %shard_map.64 = bf16[512,1024]{1,0:T(8,128)(2,1)S(1)} custom-call(bf16[512,4096]{1,0:T(8,128)(2,1)} %x_hbm.1, bf16[4096,128]{1,0:T(8,128)(2,1)} %wq_hbm.1, bf16[4096,128]{1,0:T(8,128)(2,1)} %wk_hbm.1, bf16[4096,1024]{1,0:T(8,128)(2,1)} %wv_hbm.1, bf16[1024]{0:T(1024)(128)(2,1)S(1)} %copy-done, bf16[1024,4096]{1,0:T(8,128)(2,1)} %wo_hbm.1), custom_call_target="tpu_custom_call" | custom-call | tf_op jit(solution)/shard_map/pallas_call | solution.py:416
  65.5 1.0 %copy.8 = bf16[512,1024]{1,0:T(8,128)(2,1)} copy(bf16[512,1024]{1,0:T(8,128)(2,1)S(1)} %shard_map.64) | data formatting | bytes 2097152
Async XLA Ops:
  0.0 0.7 %copy-start = (bf16[1024]{0:T(1024)(128)(2,1)S(1)}, bf16[1024]{0:T(1024)(128)(2,1)}, u32[]{:S(2)}) copy-start(bf16[1024]{0:T(1024)(128)(2,1)} %gain_ref.1) | copy-start | bytes 6148

commit v4 on v3

--- a/solution.py
+++ b/solution.py
@@ -192,7 +192,7 @@
             proj[at_rows, :] = dot(x[at_rows, :], w[i])
             return 0
 
-        lax.fori_loop(0, ROWS // TILE, rows, 0)
+        lax.fori_loop(0, ROWS // TILE, rows, 0, unroll=True)
 
         @pl.when(i == 0)
         def _():
@@ -214,7 +214,7 @@
                 states[i - 1, j] = state(head + j)
                 return 0
 
-            lax.fori_loop(0, PAIR, states_of, 0)
+            lax.fori_loop(0, PAIR, states_of, 0, unroll=True)
 
         @pl.when(i == 1)
         def _():
@@ -353,7 +353,7 @@
             z_copy(j, r).start()
             return 0
 
-        lax.fori_loop(0, 4, sent_parts, 0)
+        lax.fori_loop(0, 4, sent_parts, 0, unroll=True)
 
         def kept_parts(j, _):
             part32[j, r] = dot(norm[at_rows, :], wo[4 + j])

time: 66.5 us -> 65.3 us (0.982)
  Pallas kernels: 64.8 us -> 63.4 us
    pallas_call x1, Pallas kernels: 64.8 us -> 63.4 us  [per_device(): pl.pallas_call(kernel, out_shape=jax.ShapeDtypeStruct((ROWS, 1024), bf16)...]
where the time goes in v4:
time: 65.3 us; the launch traced here: 65 us
  Pallas kernels  63.4 us (97%)
  local copies, waits for them, and re-layouts  1.65 us (3%)
    pallas_call x1, Pallas kernels, per_device(): pl.pallas_call(kernel, out_shape=jax.ShapeDtypeStruct((ROWS, 1024), bf16)...  63.4 us
    unnamed x3, local copies, waits for them, and re-layouts  1.65 us

profile of v4, /device:TPU:1, one launch (start us, length us, event | category | flops | bytes accessed | tf_op | source)
XLA Modules:
  0.0 65.0 jit_solution(11901819911369575661)
XLA Ops:
  0.0 0.0 copy-start
  0.0 0.7 %copy-done = bf16[1024]{0:T(1024)(128)(2,1)S(1)} copy-done((bf16[1024]{0:T(1024)(128)(2,1)S(1)}, bf16[1024]{0:T(1024)(128)(2,1)}, u32[]{:S(2)}) %copy-start) | copy-done | bytes 2072
  0.7 63.4 %shard_map.64 = bf16[512,1024]{1,0:T(8,128)(2,1)S(1)} custom-call(bf16[512,4096]{1,0:T(8,128)(2,1)} %x_hbm.1, bf16[4096,128]{1,0:T(8,128)(2,1)} %wq_hbm.1, bf16[4096,128]{1,0:T(8,128)(2,1)} %wk_hbm.1, bf16[4096,1024]{1,0:T(8,128)(2,1)} %wv_hbm.1, bf16[1024]{0:T(1024)(128)(2,1)S(1)} %copy-done, bf16[1024,4096]{1,0:T(8,128)(2,1)} %wo_hbm.1), custom_call_target="tpu_custom_call" | custom-call | tf_op jit(solution)/shard_map/pallas_call | solution.py:416
  64.0 1.0 %copy.8 = bf16[512,1024]{1,0:T(8,128)(2,1)} copy(bf16[512,1024]{1,0:T(8,128)(2,1)S(1)} %shard_map.64) | data formatting | bytes 2097152
Async XLA Ops:
  0.0 0.7 %copy-start = (bf16[1024]{0:T(1024)(128)(2,1)S(1)}, bf16[1024]{0:T(1024)(128)(2,1)}, u32[]{:S(2)}) copy-start(bf16[1024]{0:T(1024)(128)(2,1)} %gain_ref.1) | copy-start | bytes 6148
